TPU v7x, 128 devices: a whole 4x4x4 slice. The times are simulated.
128 devices in a mesh: chan: 32 (over z_hi, y, x), rec: 4 (over z_lo, core).
Axes of the slice: x: 4, y: 4, z: 4 (z_hi: 2, z_lo: 2; z = z_hi * 2 + z_lo), core: 2. Of those that a mesh axis runs over, the one named last changes fastest.
Arguments:
- records: bfloat16 [4, 4096, 8192], P('rec', 'chan'), as said below
- fir_choice: int32 [8192], P('chan'), may hold values from 0 to 15
- bank: float32 [16, 64], replicated, may hold values from -4 to 4
- partner: int32 [3, 32], replicated, may hold values from 0 to 31, as said below
Outputs:
- xcorr: float32 [3, 8192, 8, 256], P(None, 'chan', 'rec')
Inputs may be any that keep to these rules, and one draw needn't show every extreme that they name: Each round is a pairing by exclusive or: partner[r, a] = a XOR m_r for one mask m_r of 1 to 31 a round, the masks of different rounds differ. `records`: samples are finite and not all zero in any channel of any record.
All inputs are finite; a program needn't handle non-finite values.
Results may differ from a plain program's by a relative error of at most 0.0055.
Values may be sent and summed in bfloat16 or wider, within the bound.
A program may use at most 128 MiB of HBM per device.

v0:
```python
import math

import jax
import jax.numpy as jnp
from jax import lax
from jax.sharding import PartitionSpec as P

LAGS = 8
ROUNDS = 3


def partner_2(x, axis, apart):
    return lax.ppermute(x, axis, [(i, i ^ 1 << apart) for i in range(lax.axis_size(axis))])


def whiten_block(raw, taps):
    length = raw.shape[0]
    width = taps.shape[1]
    signal = raw.astype(jnp.float32)
    padded = jnp.pad(signal, ((width - 1, 0), (0, 0)))
    total = jnp.zeros(signal.shape, jnp.float32)
    for tap in range(width):
        total = (
            total + taps[:, tap][None, :] * padded[width - 1 - tap : width - 1 - tap + length, :]
        )
    whitened = total.astype(jnp.bfloat16)
    values = whitened.astype(jnp.float32)
    power = jnp.mean(values * values, axis=0)
    return (values * lax.rsqrt(power + 1e-06)[None, :]).astype(jnp.bfloat16)


def lagged_term(own, mate):
    length = own.shape[0]
    padded = jnp.pad(mate, ((0, LAGS), (0, 0)))
    stacked = jnp.concatenate([padded[lag : lag + length, :] for lag in range(LAGS)], axis=1)
    product = lax.dot_general(
        own, stacked, (((0,), (0,)), ((), ())), preferred_element_type=jnp.float32
    )
    return (product * (1.0 / math.sqrt(length))).reshape(own.shape[1], LAGS, own.shape[1])


def per_device(records, fir_choice, bank, partner):
    blocks_all = lax.axis_size("chan")
    width = records.shape[2] // blocks_all
    span = records.shape[1]
    local = records[0].reshape(span, blocks_all, width)
    owned = lax.all_to_all(local, "chan", split_axis=1, concat_axis=0, tiled=True)[:, 0, :]
    onehot = (fir_choice[:, None] == jnp.arange(bank.shape[0], dtype=jnp.int32)[None, :]).astype(
        jnp.float32
    )
    taps = jnp.dot(
        onehot, bank, precision=lax.Precision.HIGHEST, preferred_element_type=jnp.float32
    )
    normed = whiten_block(owned, taps)
    terms = []
    levels = blocks_all.bit_length() - 1
    for step in range(ROUNDS):
        mask = partner[step, 0]
        moving = normed
        for level in range(levels):
            flag = jnp.bitwise_and(jnp.right_shift(mask, level), 1) == 1
            swapped = partner_2(moving, "chan", level)
            moving = jnp.where(flag, swapped, moving)
        terms.append(lagged_term(normed, moving))
    summed = [lax.psum_scatter(term, "rec", scatter_dimension=1, tiled=True) for term in terms]
    return jnp.stack(summed, axis=0)


def solution(mesh):
    placed = (P("rec", "chan", None), P("chan"), P(), P())
    return jax.shard_map(
        per_device,
        mesh=mesh,
        in_specs=placed,
        out_specs=P(None, "chan", "rec", None),
        check_vma=False,
    )
```

profile of v0, /device:TPU:0, one launch (start us, length us, event | category | flops | bytes accessed | tf_op | source)
XLA Modules:
  0.0 697.5 jit_solution(13354884076207758663)
XLA Ops:
  6.5 4.1 copy.7
  10.6 10.7 %all-to-all-start = ((bf16[128,32,256]{0,2,1:T(8,128)(2,1)}), bf16[128,32,256]{0,2,1:T(8,128)(2,1)S(1)}, u32[]{:S(2)}, u32[]{:S(2)}) async-start(bf16[128,32,256]{0,2,1:T(8,128)(2,1)} %bitcast.113), calls=%async_computation | async-start | bytes 4194304 | tf_op jit(solution)/shard_map/all_to_all | solution.py:47
  21.8 29.0 %all-to-all-done = bf16[128,32,256]{0,2,1:T(8,128)(2,1)S(1)} async-done(((bf16[128,32,256]{0,2,1:T(8,128)(2,1)}), bf16[128,32,256]{0,2,1:T(8,128)(2,1)S(1)}, u32[]{:S(2)}, u32[]{:S(2)}) %all-to-all-start) | async-done | bytes 2097184 | tf_op jit(solution)/shard_map/all_to_all | solution.py:47
  50.8 2.5 convert_bitcast_fusion
  53.3 5.6 copy.8
  58.9 137.0 %fusion = (f32[256]{0:T(256)S(1)}, bf16[4096,256]{1,0:T(8,128)(2,1)}) fusion(f32[256]{0:T(256)S(1)} %bitcast.127, f32[256]{0:T(256)S(1)} %bitcast.128, f32[256]{0:T(256)S(1)} %bitcast.129, f32[256]{0:T(256)S(1)} %bitcast.130, f32[256]{0:T(256)S(1)} %bitcast.131, f32[256]{0:T(256)S(1)} %bitcast.132, f32[256]{0:T(256)S(1)} %bitcast.133, f32[256]{0:T(256)S(1)} %bitcast.134, ...), kind=kLoop, calls=%fused_computation.2 | loop fusion | flops 137363200 | bytes 6358016 | tf_op jit(solution)/shard_map/reduce_sum | solution.py:28
  202.1 42.1 %collective-permute-done = bf16[4096,256]{1,0:T(8,128)(2,1)S(1)} collective-permute-done((bf16[4096,256]{1,0:T(8,128)(2,1)S(1)}, bf16[4096,256]{1,0:T(8,128)(2,1)S(1)}, u32[]{:S(2)}, u32[]{:S(2)}) %collective-permute-start) | collective-permute-done | bytes 2097184 | tf_op jit(solution)/shard_map/ppermute | solution.py:13
  244.7 2.5 collective-permute-start.1
  256.4 2.5 collective-permute-start.9
  258.8 36.0 %collective-permute-done.1 = bf16[4096,256]{1,0:T(8,128)(2,1)S(1)} collective-permute-done((bf16[4096,256]{1,0:T(8,128)(2,1)S(1)}, bf16[4096,256]{1,0:T(8,128)(2,1)S(1)}, u32[]{:S(2)}, u32[]{:S(2)}) %collective-permute-start.1) | collective-permute-done | bytes 2097184 | tf_op jit(solution)/shard_map/ppermute | solution.py:13
  296.0 43.9 %collective-permute-done.5 = bf16[4096,256]{1,0:T(8,128)(2,1)S(1)} collective-permute-done((bf16[4096,256]{1,0:T(8,128)(2,1)S(1)}, bf16[4096,256]{1,0:T(8,128)(2,1)S(1)}, u32[]{:S(2)}, u32[]{:S(2)}) %collective-permute-start.5) | collective-permute-done | bytes 2097184 | tf_op jit(solution)/shard_map/ppermute | solution.py:13
  340.9 40.4 %collective-permute-done.9 = bf16[4096,256]{1,0:T(8,128)(2,1)S(1)} collective-permute-done((bf16[4096,256]{1,0:T(8,128)(2,1)S(1)}, bf16[4096,256]{1,0:T(8,128)(2,1)S(1)}, u32[]{:S(2)}, u32[]{:S(2)}) %collective-permute-start.9) | collective-permute-done | bytes 2097184 | tf_op jit(solution)/shard_map/ppermute | solution.py:13
  381.5 2.7 collective-permute-start.10
  385.2 3.2 collective-permute-start.7
  388.4 42.3 %collective-permute-done.10 = bf16[4096,256]{1,0:T(8,128)(2,1)S(1)} collective-permute-done((bf16[4096,256]{1,0:T(8,128)(2,1)S(1)}, bf16[4096,256]{1,0:T(8,128)(2,1)S(1)}, u32[]{:S(2)}, u32[]{:S(2)}) %collective-permute-start.10) | collective-permute-done | bytes 2097184 | tf_op jit(solution)/shard_map/ppermute | solution.py:13
  431.5 44.6 %collective-permute-done.3 = bf16[4096,256]{1,0:T(8,128)(2,1)S(1)} collective-permute-done((bf16[4096,256]{1,0:T(8,128)(2,1)S(1)}, bf16[4096,256]{1,0:T(8,128)(2,1)S(1)}, u32[]{:S(2)}, u32[]{:S(2)}) %collective-permute-start.3) | collective-permute-done | bytes 2097184 | tf_op jit(solution)/shard_map/ppermute | solution.py:13
  478.4 42.6 %collective-permute-done.7 = bf16[4096,256]{1,0:T(8,128)(2,1)S(1)} collective-permute-done((bf16[4096,256]{1,0:T(8,128)(2,1)S(1)}, bf16[4096,256]{1,0:T(8,128)(2,1)S(1)}, u32[]{:S(2)}, u32[]{:S(2)}) %collective-permute-start.7) | collective-permute-done | bytes 2097184 | tf_op jit(solution)/shard_map/ppermute | solution.py:13
  524.6 37.8 %collective-permute-done.11 = bf16[4096,256]{1,0:T(8,128)(2,1)S(1)} collective-permute-done((bf16[4096,256]{1,0:T(8,128)(2,1)S(1)}, bf16[4096,256]{1,0:T(8,128)(2,1)S(1)}, u32[]{:S(2)}, u32[]{:S(2)}) %collective-permute-start.11) | collective-permute-done | bytes 2097184 | tf_op jit(solution)/shard_map/ppermute | solution.py:13
  570.6 4.5 convolution_multiply_fusion.2
  583.1 4.5 convolution_multiply_fusion.1
  589.5 38.2 %collective-permute-done.12 = bf16[4096,256]{1,0:T(8,128)(2,1)} collective-permute-done((bf16[4096,256]{1,0:T(8,128)(2,1)}, bf16[4096,256]{1,0:T(8,128)(2,1)}, u32[]{:S(2)}, u32[]{:S(2)}) %collective-permute-start.12) | collective-permute-done | bytes 2097184 | tf_op jit(solution)/shard_map/ppermute | solution.py:13
  633.8 4.5 convolution_multiply_fusion
  639.9 15.0 %reduce-scatter.6.cloned.1.call-done = f32[256,2,256]{2,0,1:T(8,128)} async-done(((f32[256,8,256]{2,0,1:T(8,128)}), f32[256,2,256]{2,0,1:T(8,128)}) %reduce-scatter.6.cloned.1.call-update) | async-done | bytes 524304 | tf_op jit(solution)/shard_map/reduce_scatter | solution.py:65
  654.9 31.7 %reduce-scatter.8.cloned.1.call-done = f32[256,2,256]{2,0,1:T(8,128)} async-done(((f32[256,8,256]{2,0,1:T(8,128)}), f32[256,2,256]{2,0,1:T(8,128)}) %reduce-scatter.8.cloned.1.call-update) | async-done | bytes 524304 | tf_op jit(solution)/shard_map/reduce_scatter | solution.py:65
  (77 shorter events, 45.7 us)
Async XLA Ops:
  6.5 14.9 %copy-start = (f32[16,64]{1,0:T(8,128)S(1)}, f32[16,64]{1,0:T(8,128)}, u32[]{:S(2)}) copy-start(f32[16,64]{1,0:T(8,128)} %param.6) | copy-start | bytes 12292
  6.5 14.9 %copy-start.4 = (s32[256]{0:T(256)S(1)}, s32[256]{0:T(256)}, u32[]{:S(2)}) copy-start(s32[256]{0:T(256)} %param.5) | copy-start | bytes 3076
  10.6 40.2 %all-to-all-start = ((bf16[128,32,256]{0,2,1:T(8,128)(2,1)}), bf16[128,32,256]{0,2,1:T(8,128)(2,1)S(1)}, u32[]{:S(2)}, u32[]{:S(2)}) async-start(bf16[128,32,256]{0,2,1:T(8,128)(2,1)} %bitcast.113), calls=%async_computation | async-start | bytes 4194304 | tf_op jit(solution)/shard_map/all_to_all | solution.py:47
  21.3 618.6 %reduce-scatter.4.cloned.1.call-start = ((), (), s32[]{:S(2)}) async-start(), calls=%async_computation.4 | async-start | bytes 2621440 | tf_op jit(solution)/shard_map/reduce_scatter | solution.py:65
  58.9 140.6 %copy-start.3 = (s32[3,32]{1,0:T(4,128)S(1)}, s32[3,32]{1,0:T(4,128)}, u32[]{:S(2)}) copy-start(s32[3,32]{1,0:T(4,128)} %param.7) | copy-start | bytes 1156
  195.9 48.3 %copy-start.2 = (bf16[4096,256]{1,0:T(8,128)(2,1)S(1)}, bf16[4096,256]{1,0:T(8,128)(2,1)}, u32[]{:S(2)}) copy-start(bf16[4096,256]{1,0:T(8,128)(2,1)} %get-tuple-element.12) | copy-start | bytes 6291460
  198.1 46.1 %collective-permute-start = (bf16[4096,256]{1,0:T(8,128)(2,1)S(1)}, bf16[4096,256]{1,0:T(8,128)(2,1)S(1)}, u32[]{:S(2)}, u32[]{:S(2)}) collective-permute-start(bf16[4096,256]{1,0:T(8,128)(2,1)S(1)} %fusion.1), channel_id=1, source_target_pairs={{0,4},{4,0},{8,12},{12,8},{16,20},{20,16},{24,28},{28,24},{32,36},... | collective-permute-start | bytes 6291464 | tf_op jit(solution)/shard_map/ppermute | solution.py:13
  244.7 50.1 %collective-permute-start.1 = (bf16[4096,256]{1,0:T(8,128)(2,1)S(1)}, bf16[4096,256]{1,0:T(8,128)(2,1)S(1)}, u32[]{:S(2)}, u32[]{:S(2)}) collective-permute-start(bf16[4096,256]{1,0:T(8,128)(2,1)S(1)} %get-tuple-element.13), channel_id=1, source_target_pairs={{0,8},{4,12},{8,0},{12,4},{16,24},{20,28},{24,16},{28,20},{32,40},... | collective-permute-start | bytes 6291464 | tf_op jit(solution)/shard_map/ppermute | solution.py:13
  247.2 92.6 %collective-permute-start.5 = (bf16[4096,256]{1,0:T(8,128)(2,1)S(1)}, bf16[4096,256]{1,0:T(8,128)(2,1)S(1)}, u32[]{:S(2)}, u32[]{:S(2)}) collective-permute-start(bf16[4096,256]{1,0:T(8,128)(2,1)S(1)} %get-tuple-element.15), channel_id=1, source_target_pairs={{0,8},{4,12},{8,0},{12,4},{16,24},{20,28},{24,16},{28,20},{32,40},... | collective-permute-start | bytes 6291464 | tf_op jit(solution)/shard_map/ppermute | solution.py:13
  256.4 124.9 %collective-permute-start.9 = (bf16[4096,256]{1,0:T(8,128)(2,1)S(1)}, bf16[4096,256]{1,0:T(8,128)(2,1)S(1)}, u32[]{:S(2)}, u32[]{:S(2)}) collective-permute-start(bf16[4096,256]{1,0:T(8,128)(2,1)S(1)} %get-tuple-element.14), channel_id=1, source_target_pairs={{0,8},{4,12},{8,0},{12,4},{16,24},{20,28},{24,16},{28,20},{32,40},... | collective-permute-start | bytes 6291464 | tf_op jit(solution)/shard_map/ppermute | solution.py:13
  295.2 89.1 %collective-permute-start.2 = (bf16[4096,256]{1,0:T(8,128)(2,1)S(1)}, bf16[4096,256]{1,0:T(8,128)(2,1)S(1)}, u32[]{:S(2)}, u32[]{:S(2)}) collective-permute-start(bf16[4096,256]{1,0:T(8,128)(2,1)S(1)} %broadcast_select_fusion.11), channel_id=1, source_target_pairs={{0,16},{4,20},{8,24},{12,28},{16,0},{20,4},{24,8},{28,12},{32,48},... | collective-permute-start | bytes 6291464 | tf_op jit(solution)/shard_map/ppermute | solution.py:13
  340.1 44.9 %collective-permute-start.6 = (bf16[4096,256]{1,0:T(8,128)(2,1)S(1)}, bf16[4096,256]{1,0:T(8,128)(2,1)S(1)}, u32[]{:S(2)}, u32[]{:S(2)}) collective-permute-start(bf16[4096,256]{1,0:T(8,128)(2,1)S(1)} %broadcast_select_fusion.6), channel_id=1, source_target_pairs={{0,16},{4,20},{8,24},{12,28},{16,0},{20,4},{24,8},{28,12},{32,48},... | collective-permute-start | bytes 6291464 | tf_op jit(solution)/shard_map/ppermute | solution.py:13
  381.5 49.2 %collective-permute-start.10 = (bf16[4096,256]{1,0:T(8,128)(2,1)S(1)}, bf16[4096,256]{1,0:T(8,128)(2,1)S(1)}, u32[]{:S(2)}, u32[]{:S(2)}) collective-permute-start(bf16[4096,256]{1,0:T(8,128)(2,1)S(1)} %broadcast_select_fusion.1), channel_id=1, source_target_pairs={{0,16},{4,20},{8,24},{12,28},{16,0},{20,4},{24,8},{28,12},{32,48},... | collective-permute-start | bytes 6291464 | tf_op jit(solution)/shard_map/ppermute | solution.py:13
  384.5 91.6 %collective-permute-start.3 = (bf16[4096,256]{1,0:T(8,128)(2,1)S(1)}, bf16[4096,256]{1,0:T(8,128)(2,1)S(1)}, u32[]{:S(2)}, u32[]{:S(2)}) collective-permute-start(bf16[4096,256]{1,0:T(8,128)(2,1)S(1)} %broadcast_select_fusion.12), channel_id=1, source_target_pairs={{0,32},{4,36},{8,40},{12,44},{16,48},{20,52},{24,56},{28,60},{32,0... | collective-permute-start | bytes 6291464 | tf_op jit(solution)/shard_map/ppermute | solution.py:13
  385.2 135.8 %collective-permute-start.7 = (bf16[4096,256]{1,0:T(8,128)(2,1)S(1)}, bf16[4096,256]{1,0:T(8,128)(2,1)S(1)}, u32[]{:S(2)}, u32[]{:S(2)}) collective-permute-start(bf16[4096,256]{1,0:T(8,128)(2,1)S(1)} %broadcast_select_fusion.7), channel_id=1, source_target_pairs={{0,32},{4,36},{8,40},{12,44},{16,48},{20,52},{24,56},{28,60},{32,0... | collective-permute-start | bytes 6291464 | tf_op jit(solution)/shard_map/ppermute | solution.py:13
  431.0 131.4 %collective-permute-start.11 = (bf16[4096,256]{1,0:T(8,128)(2,1)S(1)}, bf16[4096,256]{1,0:T(8,128)(2,1)S(1)}, u32[]{:S(2)}, u32[]{:S(2)}) collective-permute-start(bf16[4096,256]{1,0:T(8,128)(2,1)S(1)} %broadcast_select_fusion.2), channel_id=1, source_target_pairs={{0,32},{4,36},{8,40},{12,44},{16,48},{20,52},{24,56},{28,60},{32,0... | collective-permute-start | bytes 6291464 | tf_op jit(solution)/shard_map/ppermute | solution.py:13
  476.4 89.7 %collective-permute-start.4 = (bf16[4096,256]{1,0:T(8,128)(2,1)S(1)}, bf16[4096,256]{1,0:T(8,128)(2,1)S(1)}, u32[]{:S(2)}, u32[]{:S(2)}) collective-permute-start(bf16[4096,256]{1,0:T(8,128)(2,1)S(1)} %broadcast_select_fusion.13), channel_id=1, source_target_pairs={{0,64},{4,68},{8,72},{12,76},{16,80},{20,84},{24,88},{28,92},{32,9... | collective-permute-start | bytes 6291464 | tf_op jit(solution)/shard_map/ppermute | solution.py:13
  522.6 54.3 %collective-permute-start.8 = (bf16[4096,256]{1,0:T(8,128)(2,1)}, bf16[4096,256]{1,0:T(8,128)(2,1)}, u32[]{:S(2)}, u32[]{:S(2)}) collective-permute-start(bf16[4096,256]{1,0:T(8,128)(2,1)} %broadcast_select_fusion.8), channel_id=1, source_target_pairs={{0,64},{4,68},{8,72},{12,76},{16,80},{20,84},{24,88},{28,92},{32,9... | collective-permute-start | bytes 6291464 | tf_op jit(solution)/shard_map/ppermute | solution.py:13
  564.0 63.7 %collective-permute-start.12 = (bf16[4096,256]{1,0:T(8,128)(2,1)}, bf16[4096,256]{1,0:T(8,128)(2,1)}, u32[]{:S(2)}, u32[]{:S(2)}) collective-permute-start(bf16[4096,256]{1,0:T(8,128)(2,1)} %broadcast_select_fusion.3), channel_id=1, source_target_pairs={{0,64},{4,68},{8,72},{12,76},{16,80},{20,84},{24,88},{28,92},{32,9... | collective-permute-start | bytes 6291464 | tf_op jit(solution)/shard_map/ppermute | solution.py:13
  576.6 78.3 %reduce-scatter.6.cloned.1.call-start = ((), (), s32[]{:S(2)}) async-start(), calls=%async_computation.5 | async-start | bytes 2621440 | tf_op jit(solution)/shard_map/reduce_scatter | solution.py:65
  589.2 97.4 %reduce-scatter.8.cloned.1.call-start = ((), (), s32[]{:S(2)}) async-start(), calls=%async_computation.6 | async-start | bytes 2621440 | tf_op jit(solution)/shard_map/reduce_scatter | solution.py:65
  639.9 50.7 %copy-start.1 = (f32[16,64]{1,0:T(8,128)S(1)}, f32[16,64]{1,0:T(8,128)}, u32[]{:S(2)}) copy-start(f32[16,64]{1,0:T(8,128)} %param.6) | copy-start | bytes 12292
Sparse Core Ops, SparseCore 0:
  576.8 46.3 reduce-scatter.3
  625.7 29.2 reduce-scatter.5
  657.3 29.2 reduce-scatter.7
where the time goes:
time: 708 us; the launch traced here: 698 us
  waiting for transfers between devices  444 us (63%)
  other arithmetic  154 us (22%)
  starting transfers between devices  33.3 us (5%)
  local copies, waits for them, and re-layouts  28.8 us (4%)
  between operations  23.9 us (3%)
  matrix products  13.9 us (2%)
    ppermute x13, waiting for transfers between devices, partner_2(): lax.ppermute(x, axis, [(i, i ^ 1 << apart) for i in range(lax.axis_size(a...  368 us
    reduce_sum x1, other arithmetic, whiten_block(): power = jnp.mean(values * values, axis=0)  137 us
    reduce_scatter x3, waiting for transfers between devices, per_device(): lax.psum_scatter(term, 'rec', scatter_dimension=1, tiled=True)  46.7 us
    all_to_all x1, waiting for transfers between devices, per_device(): lax.all_to_all(local, 'chan', split_axis=1, concat_axis=0, tiled=True)  29 us
    ppermute x13, starting transfers between devices, partner_2(): lax.ppermute(x, axis, [(i, i ^ 1 << apart) for i in range(lax.axis_size(a...  22 us
  transfers between devices with their start and end apart: 17, of which 12 were waited for; matrix products, arithmetic and copies ran while one was open for 6% of the time, Pallas kernels for 0%

commit v1 on v0

v1 whole, which is shorter than its diff:
```python
import functools
import itertools

import jax
import jax.numpy as jnp
from jax import lax
from jax.experimental import pallas as pl
from jax.experimental.pallas import tpu as pltpu
from jax.sharding import PartitionSpec as P

BLOCK = 256
TAPS = 64
LAGS = 8
BANKS = 16
ROUNDS = 3
TIME = 4096
NBLK = 32
SPAN = TIME // NBLK
UNITS = ROUNDS + 1
MESH = pl.DeviceIdType.MESH


def link_loads(move):
    dz, dy, dx = move
    load = [0] * 6
    for first, step in ((0, dx), (2, dy)):
        if step in (1, 2):
            load[first] += 1
        if step in (2, 3):
            load[first + 1] += 1
    if dz:
        load[4] += 1
        load[5] += 1
    return load


def balanced_moves():
    left = [m for m in itertools.product(range(2), range(4), range(4)) if m != (0, 0, 0)]
    total = [0] * 6
    order = []

    def cost(move):
        after = [a + b for a, b in zip(total, link_loads(move))]
        return (max(after) - sum(after) / 6, -sum(link_loads(move)))

    while left:
        best = min(left, key=cost)
        left.remove(best)
        order.append(best)
        total = [a + b for a, b in zip(total, link_loads(best))]
    return order


MOVES = balanced_moves()


def whiten(raw_ref, tt_ref, choice, store):
    def body(w, acc):
        base = pl.multiple_of(w * TAPS, TAPS)
        x = raw_ref[pl.ds(base, 2 * TAPS), :]
        every = jnp.dot(
            tt_ref[...], jnp.concatenate([x, x], axis=0), preferred_element_type=jnp.float32
        )
        out = every[0:TAPS]
        for b in range(1, BANKS):
            out = jnp.where(choice == b, every[b * TAPS : (b + 1) * TAPS], out)
        rounded = out.astype(jnp.bfloat16)
        values = rounded.astype(jnp.float32)
        store(base, rounded, values)
        return acc + (values * values).reshape(TAPS // 8, 8, BLOCK).sum(0)

    acc = lax.fori_loop(0, TIME // TAPS, body, jnp.zeros((8, BLOCK), jnp.float32), unroll=4)
    return lax.rsqrt(acc.sum(0, keepdims=True) * (1.0 / TIME) + 1e-6)


def kernel(
    stage, fir_ref, mate_ref, tt_ref, out_ref,
    raw, choices, ownf, shifted, mate, keep, snd1, rcv1, snd2, rcv2,
    send_sem, recv_sem, local_sem, fir_send, fir_recv, s1_send, s1_recv, s2_send, s2_recv,
):
    me = lax.axis_index("chan")
    rec = lax.axis_index("rec")
    mz, my, mx = me // 16, (me // 4) % 4, me % 4
    core, zlo = rec % 2, rec // 2
    twin = zlo * 2 + (1 - core)
    across = (1 - zlo) * 2 + core

    def peer(move):
        dz, dy, dx = move
        return ((mz + dz) % 2) * 16 + ((my + dy) % 4) * 4 + (mx + dx) % 4

    barrier = pltpu.get_barrier_semaphore()
    for move in MOVES:
        pl.semaphore_signal(barrier, inc=1, device_id=(peer(move), rec), device_id_type=MESH)
    pl.semaphore_signal(barrier, inc=1, device_id=(me, twin), device_id_type=MESH)
    pl.semaphore_signal(barrier, inc=1, device_id=(me, across), device_id_type=MESH)
    pl.semaphore_wait(barrier, len(MOVES) + 2)

    mine = pl.ds(pl.multiple_of(TAPS + me * SPAN, TAPS), SPAN)

    def local_copy(unit):
        return pltpu.make_async_copy(stage.at[unit, me], raw.at[unit, mine], local_sem.at[unit])

    def send_unit(unit, carry):
        for move in MOVES:
            to = peer(move)
            pltpu.make_async_remote_copy(
                src_ref=stage.at[unit, to],
                dst_ref=raw.at[unit, mine],
                send_sem=send_sem.at[unit],
                recv_sem=recv_sem.at[unit],
                device_id=(to, rec),
                device_id_type=MESH,
            ).start()
        local_copy(unit).start()
        raw[unit, 0:TAPS] = jnp.zeros((TAPS, BLOCK), jnp.bfloat16)
        return carry

    for move in MOVES:
        pltpu.make_async_remote_copy(
            src_ref=fir_ref,
            dst_ref=choices.at[me],
            send_sem=fir_send,
            recv_sem=fir_recv,
            device_id=(peer(move), rec),
            device_id_type=MESH,
        ).start()
    choices[me] = fir_ref[...]
    lax.fori_loop(0, UNITS, send_unit, 0)

    def unit_wait(sem, unit):
        count = (NBLK - 1) * SPAN
        pltpu.make_async_copy(
            raw.at[unit, pl.ds(0, count)], raw.at[unit, pl.ds(0, count)], sem.at[unit]
        ).wait()

    def fir_wait(sem):
        view = choices.at[pl.ds(0, NBLK - 1)]
        pltpu.make_async_copy(view, view, sem).wait()

    ownf[0:8] = jnp.zeros((8, BLOCK), jnp.float32)
    unit_wait(recv_sem, 0)
    local_copy(0).wait()

    def store_own(base, rounded, values):
        ownf[pl.ds(base + 8, TAPS)] = values

    inv_own = whiten(raw.at[0], tt_ref, fir_ref[0:1], store_own)

    def shift(d, carry):
        base = pl.multiple_of(d * 128, 128)
        y = ownf[pl.ds(base, 136)] * inv_own
        for lag in range(LAGS):
            row = ((lag // 2) % 2) * 4 + (lag // 4) * 2 + lag % 2
            shifted[row * BLOCK : (row + 1) * BLOCK, pl.ds(base, 128)] = (
                y[8 - lag : 136 - lag].astype(jnp.bfloat16).T
            )
        return carry

    lax.fori_loop(0, TIME // 128, shift, 0, unroll=2)
    fir_wait(fir_recv)

    def store_mate(base, rounded, values):
        mate[pl.ds(base, TAPS)] = rounded

    def half(which):
        rows = pl.ds(pl.multiple_of(which * 4 * BLOCK, BLOCK), 4 * BLOCK)
        return jnp.dot(shifted[rows], mate[...], preferred_element_type=jnp.float32)

    def copy_twin(step):
        return pltpu.make_async_remote_copy(
            src_ref=snd1.at[step],
            dst_ref=rcv1.at[step],
            send_sem=s1_send.at[step],
            recv_sem=s1_recv.at[step],
            device_id=(me, twin),
            device_id_type=MESH,
        )

    def copy_across(step):
        return pltpu.make_async_remote_copy(
            src_ref=snd2.at[step],
            dst_ref=rcv2.at[step],
            send_sem=s2_send.at[step],
            recv_sem=s2_recv.at[step],
            device_id=(me, across),
            device_id_type=MESH,
        )

    def finish(step):
        copy_across(step).wait_recv()
        out_ref[step] = out_ref[step] + rcv2[step].astype(jnp.float32)

    def round_body(step, carry):
        unit_wait(recv_sem, step + 1)
        local_copy(step + 1).wait()
        which = mate_ref[step]
        choice = choices[0]
        for block in range(1, NBLK):
            choice = jnp.where(which == block, choices[block], choice)
        choice = choice[0:1]
        scale = whiten(raw.at[step + 1], tt_ref, choice, store_mate) * (TIME**-0.5)
        snd1[step] = (half(1 - core) * scale).astype(jnp.bfloat16).reshape(2, 2 * BLOCK, BLOCK)
        copy_twin(step).start()
        keep[...] = (half(core) * scale).reshape(2, 2 * BLOCK, BLOCK)
        copy_twin(step).wait_recv()
        snd2[step] = (keep[1 - zlo] + rcv1[step, 1 - zlo].astype(jnp.float32)).astype(jnp.bfloat16)
        copy_across(step).start()
        out_ref[step] = keep[zlo] + rcv1[step, zlo].astype(jnp.float32)

        @pl.when(step > 0)
        def _():
            finish(step - 1)

        return carry

    lax.fori_loop(0, ROUNDS, round_body, 0)
    finish(ROUNDS - 1)
    fir_wait(fir_send)
    for unit in range(UNITS):
        unit_wait(send_sem, unit)
    for step in range(ROUNDS):
        copy_twin(step).wait_send()
        copy_across(step).wait_send()


def prepare_kernel(part_ref, fir_in, bank_ref, rec_ref, stage_ref, fir_ref, mate_ref, tt_ref):
    unit = pl.program_id(0)
    for to in range(NBLK):
        which = jnp.where(unit == 0, to, part_ref[jnp.maximum(unit - 1, 0), to])
        stage_ref[0, to] = rec_ref[:, pl.ds(pl.multiple_of(which * BLOCK, BLOCK), BLOCK)]

    @pl.when(unit == 0)
    def _():
        fir_ref[...] = jnp.broadcast_to(fir_in[...], (8, BLOCK))
        me = lax.axis_index("chan")
        for step in range(ROUNDS):
            mate_ref[step] = jnp.full((8, BLOCK), part_ref[step, me], jnp.int32)
        tap = lax.broadcasted_iota(jnp.int32, (TAPS, 256), 0)
        lane = lax.broadcasted_iota(jnp.int32, (TAPS, 256), 1)
        flip = (tap + lane == TAPS).astype(jnp.float32)
        turned = jnp.dot(
            bank_ref[...], flip, precision=lax.Precision.HIGHEST, preferred_element_type=jnp.float32
        )
        for b in range(BANKS):
            row = jnp.broadcast_to(turned[b : b + 1, :], (TAPS, 256))
            t = pltpu.roll(row, 0, 1, stride=1, stride_axis=0)[:, : 2 * TAPS]
            high = t.astype(jnp.bfloat16)
            low = (t - high.astype(jnp.float32)).astype(jnp.bfloat16)
            tt_ref[b * TAPS : (b + 1) * TAPS, :] = jnp.concatenate([high, low], axis=1)


def prepare(records, fir_choice, bank, partner):
    def whole(*shape):
        return pl.BlockSpec(shape, lambda u, *_: (0,) * len(shape))

    return pl.pallas_call(
        prepare_kernel,
        grid_spec=pltpu.PrefetchScalarGridSpec(
            num_scalar_prefetch=1,
            grid=(UNITS,),
            in_specs=[whole(1, BLOCK), whole(BANKS, TAPS), whole(SPAN, NBLK * BLOCK)],
            out_specs=[
                pl.BlockSpec((1, NBLK, SPAN, BLOCK), lambda u, *_: (u, 0, 0, 0)),
                whole(8, BLOCK),
                whole(ROUNDS, 8, BLOCK),
                whole(BANKS * TAPS, 256),
            ],
        ),
        out_shape=[
            jax.ShapeDtypeStruct((UNITS, NBLK, SPAN, BLOCK), jnp.bfloat16),
            jax.ShapeDtypeStruct((8, BLOCK), jnp.int32),
            jax.ShapeDtypeStruct((ROUNDS, 8, BLOCK), jnp.int32),
            jax.ShapeDtypeStruct((BANKS * TAPS, 256), jnp.bfloat16),
        ],
        compiler_params=pltpu.CompilerParams(vmem_limit_bytes=24 << 20),
        name="prepare",
    )(partner, fir_choice[None, :], bank, records)


def per_device(records, fir_choice, bank, partner):
    ready = prepare(records[0], fir_choice, bank, partner)
    vmem = pl.BlockSpec(memory_space=pltpu.VMEM)
    bf16, f32 = jnp.bfloat16, jnp.float32
    dma = pltpu.SemaphoreType.DMA
    out = pl.pallas_call(
        kernel,
        out_shape=jax.ShapeDtypeStruct((ROUNDS, 2 * BLOCK, BLOCK), f32),
        in_specs=[pl.BlockSpec(memory_space=pl.ANY), vmem, vmem, vmem],
        out_specs=vmem,
        scratch_shapes=[
            pltpu.VMEM((UNITS, TAPS + TIME, BLOCK), bf16),
            pltpu.VMEM((NBLK, 8, BLOCK), jnp.int32),
            pltpu.VMEM((8 + TIME, BLOCK), f32),
            pltpu.VMEM((LAGS * BLOCK, TIME), bf16),
            pltpu.VMEM((TIME, BLOCK), bf16),
            pltpu.VMEM((2, 2 * BLOCK, BLOCK), f32),
            pltpu.VMEM((ROUNDS, 2, 2 * BLOCK, BLOCK), bf16),
            pltpu.VMEM((ROUNDS, 2, 2 * BLOCK, BLOCK), bf16),
            pltpu.VMEM((ROUNDS, 2 * BLOCK, BLOCK), bf16),
            pltpu.VMEM((ROUNDS, 2 * BLOCK, BLOCK), bf16),
            dma((UNITS,)), dma((UNITS,)), dma((UNITS,)), dma, dma,
            dma((ROUNDS,)), dma((ROUNDS,)), dma((ROUNDS,)), dma((ROUNDS,)),
        ],
        compiler_params=pltpu.CompilerParams(
            collective_id=0, has_side_effects=True, vmem_limit_bytes=60 << 20
        ),
        name="correlate",
    )(*ready)
    return out.reshape(ROUNDS, 2, BLOCK, BLOCK).transpose(0, 2, 1, 3)


def solution(mesh):
    placed = (P("rec", "chan", None), P("chan"), P(), P())
    return jax.shard_map(
        per_device,
        mesh=mesh,
        in_specs=placed,
        out_specs=P(None, "chan", "rec", None),
        check_vma=False,
    )
```

time: 708 us -> 158 us (0.22); the launches traced: 698 us -> 155 us
  waiting for transfers between devices: 444 us -> 0 us
  other arithmetic: 154 us -> 0 us
  Pallas kernels: 0 us -> 142 us
  starting transfers between devices: 33.3 us -> 0 us
  between operations: 23.9 us -> 0.03 us
  local copies, waits for them, and re-layouts: 28.8 us -> 12.6 us
  matrix products: 13.9 us -> 0 us
    ppermute x13 -> x0, waiting for transfers between devices: 368 us -> none  [partner_2(): lax.ppermute(x, axis, [(i, i ^ 1 << apart) for i in range(lax.axis_size(a...]
    pallas_call x0 -> x2, Pallas kernels: none -> 142 us  [the longest x1 140 us: per_device(): pl.pallas_call(kernel, out_shape=jax.ShapeDtypeStruct((ROUNDS, 2 * BLOCK,...]
    reduce_sum x1 -> x0, other arithmetic: 137 us -> none  [whiten_block(): power = jnp.mean(values * values, axis=0)]
    reduce_scatter x3 -> x0, waiting for transfers between devices: 46.7 us -> none  [per_device(): lax.psum_scatter(term, 'rec', scatter_dimension=1, tiled=True)]
    all_to_all x1 -> x0, waiting for transfers between devices: 29 us -> none  [per_device(): lax.all_to_all(local, 'chan', split_axis=1, concat_axis=0, tiled=True)]
    ppermute x13 -> x0, starting transfers between devices: 22 us -> none  [partner_2(): lax.ppermute(x, axis, [(i, i ^ 1 << apart) for i in range(lax.axis_size(a...]
    dot_general x4 -> x0, matrix products: 13.9 us -> none  [the longest x3 13.6 us: lagged_term(): lax.dot_general(own, stacked, (((0,), (0,)), ((), ())), preferred_element...]
    all_to_all x1 -> x0, starting transfers between devices: 10.7 us -> none  [per_device(): lax.all_to_all(local, 'chan', split_axis=1, concat_axis=0, tiled=True)]
  transfers between devices with their start and end apart: 17 -> 0, of which waited for: 12 -> 0; matrix products, arithmetic and copies ran while one was open for 6% -> 0% of each run, Pallas kernels for 0% -> 0%
where the time goes in v1:
time: 158 us; the launch traced here: 155 us
  Pallas kernels  142 us (90%)
  local copies, waits for them, and re-layouts  12.6 us (8%)
    pallas_call x1, Pallas kernels, per_device(): pl.pallas_call(kernel, out_shape=jax.ShapeDtypeStruct((ROUNDS, 2 * BLOCK,...  140 us
    unnamed x16, local copies, waits for them, and re-layouts  8.87 us
    reshape x1, local copies, waits for them, and re-layouts, per_device(): return out.reshape(ROUNDS, 2, BLOCK, BLOCK).transpose(0, 2, 1, 3)  3.76 us

profile of v1, /device:TPU:0, one launch (start us, length us, event | category | flops | bytes accessed | tf_op | source)
XLA Modules:
  0.0 154.9 jit_solution(5733032272729364652)
XLA Ops:
  0.0 0.0 copy-start.1
  0.0 1.6 %copy-done.1 = bf16[1,128,8192]{2,1,0:T(8,128)(2,1)S(1)} copy-done((bf16[1,128,8192]{2,1,0:T(8,128)(2,1)S(1)}, bf16[1,128,8192]{2,1,0:T(8,128)(2,1)}, u32[]{:S(2)}) %copy-start.1) | copy-done | bytes 2097176
  1.6 0.0 copy-start.4
  1.6 0.7 copy-done.4
  2.3 0.0 copy-start.6
  2.3 0.7 copy-done.6
  3.0 0.0 copy-start.7
  3.0 0.7 copy-done.7
  3.7 2.2 %prepare.1 = (bf16[4,32,128,256]{3,2,1,0:T(8,128)(2,1)S(1)}, s32[8,256]{1,0:T(8,128)S(1)}, s32[3,8,256]{2,1,0:T(8,128)S(1)}, bf16[1024,256]{1,0:T(8,128)(2,1)S(1)}) custom-call(s32[3,32]{1,0:T(4,128)S(1)} %copy-done.6, s32[1,256]{1,0:T(1,128)S(1)} %bitcast.7, f32[16,64]{1,0:T(8,128)S(1)} %copy-done.4, bf16[128,8192]{1,0:T(8,128)(2,1)S(1)} %bitcast.6), custom_call_target="tpu_custom_call" | custom-call | tf_op jit(solution)/shard_map/prepare/pallas_call | solution.py:257
  5.9 0.0 copy-start
  5.9 3.2 %copy-done = bf16[4,32,128,256]{3,2,1,0:T(8,128)(2,1)} copy-done((bf16[4,32,128,256]{3,2,1,0:T(8,128)(2,1)}, bf16[4,32,128,256]{3,2,1,0:T(8,128)(2,1)S(1)}, u32[]{:S(2)}) %copy-start) | copy-done | bytes 8388632
  9.1 0.0 copy-start.2
  9.1 0.8 copy-done.2
  9.9 0.0 copy-start.3
  9.9 0.6 copy-done.3
  10.5 0.0 copy-start.5
  10.5 0.6 copy-done.5
  11.1 140.0 %correlate.1 = f32[3,512,256]{2,1,0:T(8,128)} custom-call(bf16[4,32,128,256]{3,2,1,0:T(8,128)(2,1)} %copy-done, s32[8,256]{1,0:T(8,128)} %copy-done.5, s32[3,8,256]{2,1,0:T(8,128)} %copy-done.3, bf16[1024,256]{1,0:T(8,128)(2,1)} %copy-done.2), custom_call_target="tpu_custom_call" | custom-call | tf_op jit(solution)/shard_map/correlate/pallas_call | solution.py:286
  151.1 3.8 %copy.7 = f32[3,2,256,256]{3,1,2,0:T(2,128)} copy(f32[3,2,256,256]{3,2,1,0:T(8,128)} %bitcast.8) | data formatting | bytes 3145728 | tf_op jit(solution)/shard_map/reshape | solution.py:310
Async XLA Ops:
  0.0 1.6 %copy-start.1 = (bf16[1,128,8192]{2,1,0:T(8,128)(2,1)S(1)}, bf16[1,128,8192]{2,1,0:T(8,128)(2,1)}, u32[]{:S(2)}) copy-start(bf16[1,128,8192]{2,1,0:T(8,128)(2,1)} %param.4) | copy-start | bytes 6291460
  1.6 0.7 copy-start.4
  2.3 0.7 copy-start.6
  3.0 0.7 copy-start.7
  5.9 3.2 %copy-start = (bf16[4,32,128,256]{3,2,1,0:T(8,128)(2,1)}, bf16[4,32,128,256]{3,2,1,0:T(8,128)(2,1)S(1)}, u32[]{:S(2)}) copy-start(bf16[4,32,128,256]{3,2,1,0:T(8,128)(2,1)S(1)} %get-tuple-element.9.stage) | copy-start | bytes 25165828
  9.1 0.8 copy-start.2
  9.9 0.6 copy-start.3
  10.5 0.6 copy-start.5

commit v2 on v1

v2 whole, which is shorter than its diff:
```python
import itertools

import jax
import jax.numpy as jnp
from jax import lax
from jax.experimental import pallas as pl
from jax.experimental.pallas import tpu as pltpu
from jax.sharding import PartitionSpec as P

BLOCK = 256
TAPS = 64
LAGS = 8
BANKS = 16
ROUNDS = 3
TIME = 4096
NBLK = 32
SPAN = TIME // NBLK
UNITS = ROUNDS + 1
MESH = pl.DeviceIdType.MESH


def row_pairs():
    groups = []
    for j in range(4):
        dz, dy = j // 2, j % 2
        group = []
        for first, second in ((1, 3), (3, 1), (2, 2), (0, 0)):
            group.append((1 - dz, dy + 2, first))
            group.append((dz, dy, second))
        groups.append(group)
    return groups


GROUPS = row_pairs()
MOVES = [(j, move) for j, group in enumerate(GROUPS) for move in group if move != (0, 0, 0)]


def whiten(raw_ref, tt_ref, choice, ready, store):
    def window(w, acc):
        base = pl.multiple_of(w * TAPS, TAPS)
        x = raw_ref[pl.ds(base, 2 * TAPS), :]
        every = jnp.dot(
            tt_ref[...], jnp.concatenate([x, x], axis=0), preferred_element_type=jnp.float32
        )
        out = every[0:TAPS]
        for b in range(1, BANKS):
            out = jnp.where(choice == b, every[b * TAPS : (b + 1) * TAPS], out)
        rounded = out.astype(jnp.bfloat16)
        values = rounded.astype(jnp.float32)
        store(base, rounded, values)
        return acc + (values * values).reshape(TAPS // 8, 8, BLOCK).sum(0)

    def group(j, acc):
        for row in ready(j):
            for inner in range(1, 8):
                acc = window(row * 8 + inner, acc)
        return acc

    acc = lax.fori_loop(0, len(GROUPS), group, jnp.zeros((8, BLOCK), jnp.float32))
    for row in range(NBLK // 4):
        acc = window(row * 8, acc)
    return lax.rsqrt(acc.sum(0, keepdims=True) * (1.0 / TIME) + 1e-6)


def kernel(
    stage, fir_ref, mate_ref, tt_ref, out_ref,
    raw, choices, ownf, shifted, mate, keep, snd1, rcv1, snd2, rcv2,
    send_sem, recv_sem, local_sem, fir_send, fir_recv, s1_send, s1_recv, s2_send, s2_recv,
):
    me = lax.axis_index("chan")
    rec = lax.axis_index("rec")
    mz, my, mx = me // 16, (me // 4) % 4, me % 4
    core, zlo = rec % 2, rec // 2
    twin = zlo * 2 + (1 - core)
    across = (1 - zlo) * 2 + core

    turn = 1 - 2 * core

    def peer(move):
        dz, dy, dx = move
        return ((mz + dz) % 2) * 16 + ((my + 4 + turn * dy) % 4) * 4 + (mx + 4 + turn * dx) % 4

    barrier = pltpu.get_barrier_semaphore()
    for _, move in MOVES:
        pl.semaphore_signal(barrier, inc=1, device_id=(peer(move), rec), device_id_type=MESH)
    pl.semaphore_signal(barrier, inc=1, device_id=(me, twin), device_id_type=MESH)
    pl.semaphore_signal(barrier, inc=1, device_id=(me, across), device_id_type=MESH)
    pl.semaphore_wait(barrier, len(MOVES) + 2)

    mine = pl.ds(pl.multiple_of(TAPS + me * SPAN, TAPS), SPAN)

    def local_copy(unit):
        return pltpu.make_async_copy(stage.at[unit, me], raw.at[unit, mine], local_sem.at[unit])

    def send_unit(unit, carry):
        for j, move in MOVES:
            to = peer(move)
            pltpu.make_async_remote_copy(
                src_ref=stage.at[unit, to],
                dst_ref=raw.at[unit, mine],
                send_sem=send_sem.at[unit],
                recv_sem=recv_sem.at[unit, j],
                device_id=(to, rec),
                device_id_type=MESH,
            ).start()
        local_copy(unit).start()
        raw[unit, 0:TAPS] = jnp.zeros((TAPS, BLOCK), jnp.bfloat16)
        return carry

    for _, move in MOVES:
        pltpu.make_async_remote_copy(
            src_ref=fir_ref,
            dst_ref=choices.at[me],
            send_sem=fir_send,
            recv_sem=fir_recv,
            device_id=(peer(move), rec),
            device_id_type=MESH,
        ).start()
    choices[me] = fir_ref[...]
    lax.fori_loop(0, UNITS, send_unit, 0)

    def bytes_wait(sem, pieces):
        view = raw.at[0, pl.ds(0, pieces * SPAN)]
        pltpu.make_async_copy(view, view, sem).wait()

    def arrival(unit):
        def ready(j):
            dz, dy = j // 2, j % 2

            @pl.when(j == 0)
            def _():
                bytes_wait(recv_sem.at[unit, j], 7)
                local_copy(unit).wait()

            @pl.when(j > 0)
            def _():
                bytes_wait(recv_sem.at[unit, j], 8)

            first = ((mz + dz) % 2) * 4 + (my + 4 - turn * dy) % 4
            second = ((mz + 1 - dz) % 2) * 4 + (my + 8 - turn * (dy + 2)) % 4
            return first, second

        return ready

    def fir_wait(sem):
        view = choices.at[pl.ds(0, NBLK - 1)]
        pltpu.make_async_copy(view, view, sem).wait()

    ownf[0:8] = jnp.zeros((8, BLOCK), jnp.float32)

    def store_own(base, rounded, values):
        ownf[pl.ds(base + 8, TAPS)] = values

    inv_own = whiten(raw.at[0], tt_ref, fir_ref[0:1], arrival(0), store_own)

    def shift(d, carry):
        base = pl.multiple_of(d * 128, 128)
        y = ownf[pl.ds(base, 136)] * inv_own
        for lag in range(LAGS):
            row = ((lag // 2) % 2) * 4 + (lag // 4) * 2 + lag % 2
            shifted[row * BLOCK : (row + 1) * BLOCK, pl.ds(base, 128)] = (
                y[8 - lag : 136 - lag].astype(jnp.bfloat16).T
            )
        return carry

    lax.fori_loop(0, TIME // 128, shift, 0, unroll=2)
    fir_wait(fir_recv)

    def store_mate(base, rounded, values):
        mate[pl.ds(base, TAPS)] = rounded

    def quarter(to_core, to_zlo):
        rows = pl.ds(pl.multiple_of((to_core * 2 + to_zlo) * 2 * BLOCK, BLOCK), 2 * BLOCK)
        return jnp.dot(shifted[rows], mate[...], preferred_element_type=jnp.float32)

    def copy_twin(step, part):
        return pltpu.make_async_remote_copy(
            src_ref=snd1.at[step, part],
            dst_ref=rcv1.at[step, part],
            send_sem=s1_send.at[step, part],
            recv_sem=s1_recv.at[step, part],
            device_id=(me, twin),
            device_id_type=MESH,
        )

    def copy_across(step):
        return pltpu.make_async_remote_copy(
            src_ref=snd2.at[step],
            dst_ref=rcv2.at[step],
            send_sem=s2_send.at[step],
            recv_sem=s2_recv.at[step],
            device_id=(me, across),
            device_id_type=MESH,
        )

    def finish(step):
        copy_across(step).wait_recv()
        out_ref[step] = out_ref[step] + rcv2[step].astype(jnp.float32)

    def round_body(step, carry):
        which = mate_ref[step]
        choice = choices[0]
        for block in range(1, NBLK):
            choice = jnp.where(which == block, choices[block], choice)
        choice = choice[0:1]
        inv = whiten(raw.at[step + 1], tt_ref, choice, arrival(step + 1), store_mate)
        scale = inv * (TIME**-0.5)
        for part, target in ((0, 1 - zlo), (1, zlo)):
            snd1[step, part] = (quarter(1 - core, target) * scale).astype(jnp.bfloat16)
            copy_twin(step, part).start()
            keep[...] = quarter(core, target) * scale
            copy_twin(step, part).wait_recv()
            both = keep[...] + rcv1[step, part].astype(jnp.float32)
            if part == 0:
                snd2[step] = both.astype(jnp.bfloat16)
                copy_across(step).start()
            else:
                out_ref[step] = both

        @pl.when(step > 0)
        def _():
            finish(step - 1)

        return carry

    lax.fori_loop(0, ROUNDS, round_body, 0)
    finish(ROUNDS - 1)
    fir_wait(fir_send)
    for unit in range(UNITS):
        bytes_wait(send_sem.at[unit], NBLK - 1)
    for step in range(ROUNDS):
        copy_twin(step, 0).wait_send()
        copy_twin(step, 1).wait_send()
        copy_across(step).wait_send()


def prepare_kernel(
    part_hbm, fir_hbm, bank_hbm, rec_hbm, stage_ref, fir_ref, mate_ref, tt_ref,
    part_ref, fir_in, bank_ref, rec_ref, sem, rec_sem,
):
    slices = rec_sem.shape[0]
    rows = SPAN // slices
    small = [
        pltpu.make_async_copy(source, target, sem.at[i])
        for i, (source, target) in enumerate(
            ((part_hbm, part_ref), (bank_hbm, bank_ref), (fir_hbm, fir_in))
        )
    ]
    large = [
        pltpu.make_async_copy(
            rec_hbm.at[pl.ds(i * rows, rows)], rec_ref.at[pl.ds(i * rows, rows)], rec_sem.at[i]
        )
        for i in range(slices)
    ]
    for copy in small + large:
        copy.start()
    for copy in small:
        copy.wait()

    fir_ref[...] = jnp.broadcast_to(fir_in[...], (8, BLOCK))
    me = lax.axis_index("chan")
    for step in range(ROUNDS):
        mate_ref[step] = jnp.full((8, BLOCK), part_ref[step, me], jnp.int32)
    tap = lax.broadcasted_iota(jnp.int32, (TAPS, 256), 0)
    lane = lax.broadcasted_iota(jnp.int32, (TAPS, 256), 1)
    flip = (tap + lane == TAPS).astype(jnp.float32)
    turned = jnp.dot(
        bank_ref[...], flip, precision=lax.Precision.HIGHEST, preferred_element_type=jnp.float32
    )
    for b in range(BANKS):
        row = jnp.broadcast_to(turned[b : b + 1, :], (TAPS, 256))
        t = pltpu.roll(row, 0, 1, stride=1, stride_axis=0)[:, : 2 * TAPS]
        high = t.astype(jnp.bfloat16)
        low = (t - high.astype(jnp.float32)).astype(jnp.bfloat16)
        tt_ref[b * TAPS : (b + 1) * TAPS, :] = jnp.concatenate([high, low], axis=1)

    for i in range(slices):
        large[i].wait()
        cut = slice(i * rows, (i + 1) * rows)
        for to in range(NBLK):
            stage_ref[0, to, cut] = rec_ref[cut, to * BLOCK : (to + 1) * BLOCK]
            for step in range(ROUNDS):
                start = pl.multiple_of(part_ref[step, to] * BLOCK, BLOCK)
                stage_ref[step + 1, to, cut] = rec_ref[cut, pl.ds(start, BLOCK)]


def prepare(records, fir_choice, bank, partner):
    hbm = pl.BlockSpec(memory_space=pltpu.HBM)
    vmem = pl.BlockSpec(memory_space=pltpu.VMEM)
    slices = 2
    return pl.pallas_call(
        prepare_kernel,
        in_specs=[hbm] * 4,
        out_specs=[vmem] * 4,
        out_shape=[
            jax.ShapeDtypeStruct((UNITS, NBLK, SPAN, BLOCK), jnp.bfloat16),
            jax.ShapeDtypeStruct((8, BLOCK), jnp.int32),
            jax.ShapeDtypeStruct((ROUNDS, 8, BLOCK), jnp.int32),
            jax.ShapeDtypeStruct((BANKS * TAPS, 256), jnp.bfloat16),
        ],
        scratch_shapes=[
            pltpu.SMEM((ROUNDS, NBLK), jnp.int32),
            pltpu.VMEM((1, BLOCK), jnp.int32),
            pltpu.VMEM((BANKS, TAPS), jnp.float32),
            pltpu.VMEM((SPAN, NBLK * BLOCK), jnp.bfloat16),
            pltpu.SemaphoreType.DMA((3,)),
            pltpu.SemaphoreType.DMA((slices,)),
        ],
        compiler_params=pltpu.CompilerParams(vmem_limit_bytes=14 << 20),
        name="prepare",
    )(partner, fir_choice[None, :], bank, records)


def per_device(records, fir_choice, bank, partner):
    ready = prepare(records[0], fir_choice, bank, partner)
    vmem = pl.BlockSpec(memory_space=pltpu.VMEM)
    bf16, f32 = jnp.bfloat16, jnp.float32
    dma = pltpu.SemaphoreType.DMA
    out = pl.pallas_call(
        kernel,
        out_shape=jax.ShapeDtypeStruct((ROUNDS, 2 * BLOCK, BLOCK), f32),
        in_specs=[pl.BlockSpec(memory_space=pl.ANY), vmem, vmem, vmem],
        out_specs=vmem,
        scratch_shapes=[
            pltpu.VMEM((UNITS, TAPS + TIME, BLOCK), bf16),
            pltpu.VMEM((NBLK, 8, BLOCK), jnp.int32),
            pltpu.VMEM((8 + TIME, BLOCK), f32),
            pltpu.VMEM((LAGS * BLOCK, TIME), bf16),
            pltpu.VMEM((TIME, BLOCK), bf16),
            pltpu.VMEM((2 * BLOCK, BLOCK), f32),
            pltpu.VMEM((ROUNDS, 2, 2 * BLOCK, BLOCK), bf16),
            pltpu.VMEM((ROUNDS, 2, 2 * BLOCK, BLOCK), bf16),
            pltpu.VMEM((ROUNDS, 2 * BLOCK, BLOCK), bf16),
            pltpu.VMEM((ROUNDS, 2 * BLOCK, BLOCK), bf16),
            dma((UNITS,)), dma((UNITS, len(GROUPS))), dma((UNITS,)), dma, dma,
            dma((ROUNDS, 2)), dma((ROUNDS, 2)), dma((ROUNDS,)), dma((ROUNDS,)),
        ],
        compiler_params=pltpu.CompilerParams(
            collective_id=0, has_side_effects=True, vmem_limit_bytes=40 << 20
        ),
        name="correlate",
    )(*ready)
    return out.reshape(ROUNDS, 2, BLOCK, BLOCK).transpose(0, 2, 1, 3)


def solution(mesh):
    placed = (P("rec", "chan", None), P("chan"), P(), P())
    return jax.shard_map(
        per_device,
        mesh=mesh,
        in_specs=placed,
        out_specs=P(None, "chan", "rec", None),
        check_vma=False,
    )
```

time: 158 us -> 139 us (0.88); the launches traced: 155 us -> 139 us
  Pallas kernels: 142 us -> 133 us
  local copies, waits for them, and re-layouts: 12.6 us -> 6 us
    pallas_call x1, Pallas kernels: 140 us -> 131 us  [per_device(): pl.pallas_call(kernel, out_shape=jax.ShapeDtypeStruct((ROUNDS, 2 * BLOCK,...]
    unnamed x16 -> x8, local copies, waits for them, and re-layouts: 8.87 us -> 3.65 us
where the time goes in v2:
time: 139 us
  Pallas kernels  133 us (96%)
  local copies, waits for them, and re-layouts  6 us (4%)
    pallas_call x1, Pallas kernels, per_device(): pl.pallas_call(kernel, out_shape=jax.ShapeDtypeStruct((ROUNDS, 2 * BLOCK,...  131 us
    unnamed x8, local copies, waits for them, and re-layouts  3.65 us

profile of v2, /device:TPU:0, one launch (start us, length us, event | category | flops | bytes accessed | tf_op | source)
XLA Modules:
  0.0 139.3 jit_solution(17281179395793399891)
XLA Ops:
  0.0 0.0 copy-start
  0.0 1.6 %copy-done = bf16[1,128,8192]{2,1,0:T(8,128)(2,1)S(1)} copy-done((bf16[1,128,8192]{2,1,0:T(8,128)(2,1)S(1)}, bf16[1,128,8192]{2,1,0:T(8,128)(2,1)}, u32[]{:S(2)}) %copy-start) | copy-done | bytes 2097176
  1.6 0.0 copy-start.1
  1.6 0.7 copy-done.1
  2.3 0.0 copy-start.2
  2.3 0.7 copy-done.2
  3.0 0.0 copy-start.3
  3.0 0.7 copy-done.3
  3.7 2.0 %prepare.1 = (bf16[4,32,128,256]{3,2,1,0:T(8,128)(2,1)S(1)}, s32[8,256]{1,0:T(8,128)S(1)}, s32[3,8,256]{2,1,0:T(8,128)S(1)}, bf16[1024,256]{1,0:T(8,128)(2,1)S(1)}) custom-call(s32[3,32]{1,0:T(4,128)S(1)} %copy-done.2, s32[1,256]{1,0:T(1,128)S(1)} %bitcast.8, f32[16,64]{1,0:T(8,128)S(1)} %copy-done.1, bf16[128,8192]{1,0:T(8,128)(2,1)S(1)} %bitcast.7), custom_call_target="tpu_custom_call" | custom-call | tf_op jit(solution)/shard_map/prepare/pallas_call | solution.py:291
  5.7 131.2 %correlate.1 = f32[3,512,256]{2,1,0:T(8,128)S(1)} custom-call(bf16[4,32,128,256]{3,2,1,0:T(8,128)(2,1)S(1)} %get-tuple-element.9.stage, s32[8,256]{1,0:T(8,128)S(1)} %get-tuple-element.10.fir_ref, s32[3,8,256]{2,1,0:T(8,128)S(1)} %get-tuple-element.11.mate_ref, bf16[1024,256]{1,0:T(8,128)(2,1)S(1)} %get-tuple-element.12.tt_ref), custom_call_target="tpu_custom_call" | custom-call | tf_op jit(solution)/shard_map/correlate/pallas_call | solution.py:319
  136.9 2.4 %copy.7 = f32[3,2,256,256]{3,1,2,0:T(2,128)} copy(f32[3,2,256,256]{3,2,1,0:T(8,128)S(1)} %bitcast.6) | data formatting | bytes 3145728 | tf_op jit(solution)/shard_map/reshape | solution.py:343
Async XLA Ops:
  0.0 1.6 %copy-start = (bf16[1,128,8192]{2,1,0:T(8,128)(2,1)S(1)}, bf16[1,128,8192]{2,1,0:T(8,128)(2,1)}, u32[]{:S(2)}) copy-start(bf16[1,128,8192]{2,1,0:T(8,128)(2,1)} %param.4) | copy-start | bytes 6291460
  1.6 0.7 copy-start.1
  2.3 0.7 copy-start.2
  3.0 0.7 copy-start.3

commit v3 on v2

--- a/solution.py
+++ b/solution.py
@@ -107,6 +107,7 @@
         raw[unit, 0:TAPS] = jnp.zeros((TAPS, BLOCK), jnp.bfloat16)
         return carry
 
+    send_unit(0, 0)
     for _, move in MOVES:
         pltpu.make_async_remote_copy(
             src_ref=fir_ref,
@@ -117,7 +118,7 @@
             device_id_type=MESH,
         ).start()
     choices[me] = fir_ref[...]
-    lax.fori_loop(0, UNITS, send_unit, 0)
+    lax.fori_loop(1, UNITS, send_unit, 0)
 
     def bytes_wait(sem, pieces):
         view = raw.at[0, pl.ds(0, pieces * SPAN)]
@@ -169,33 +170,41 @@
     def store_mate(base, rounded, values):
         mate[pl.ds(base, TAPS)] = rounded
 
-    def quarter(to_core, to_zlo):
-        rows = pl.ds(pl.multiple_of((to_core * 2 + to_zlo) * 2 * BLOCK, BLOCK), 2 * BLOCK)
+    def product(to_core, to_zlo, first, count):
+        start = ((to_core * 2 + to_zlo) * 2 + first) * BLOCK
+        rows = pl.ds(pl.multiple_of(start, BLOCK), count * BLOCK)
         return jnp.dot(shifted[rows], mate[...], preferred_element_type=jnp.float32)
 
     def copy_twin(step, part):
+        if part == 2:
+            where = (step, 1)
+        else:
+            where = (step, 0, pl.ds(part * BLOCK, BLOCK))
         return pltpu.make_async_remote_copy(
-            src_ref=snd1.at[step, part],
-            dst_ref=rcv1.at[step, part],
+            src_ref=snd1.at[where],
+            dst_ref=rcv1.at[where],
             send_sem=s1_send.at[step, part],
             recv_sem=s1_recv.at[step, part],
             device_id=(me, twin),
             device_id_type=MESH,
         )
 
-    def copy_across(step):
+    def copy_across(step, lag):
+        where = (step, pl.ds(lag * BLOCK, BLOCK))
         return pltpu.make_async_remote_copy(
-            src_ref=snd2.at[step],
-            dst_ref=rcv2.at[step],
-            send_sem=s2_send.at[step],
-            recv_sem=s2_recv.at[step],
+            src_ref=snd2.at[where],
+            dst_ref=rcv2.at[where],
+            send_sem=s2_send.at[step, lag],
+            recv_sem=s2_recv.at[step, lag],
             device_id=(me, across),
             device_id_type=MESH,
         )
 
     def finish(step):
-        copy_across(step).wait_recv()
-        out_ref[step] = out_ref[step] + rcv2[step].astype(jnp.float32)
+        for lag in range(2):
+            here = slice(lag * BLOCK, (lag + 1) * BLOCK)
+            copy_across(step, lag).wait_recv()
+            out_ref[step, here] = out_ref[step, here] + rcv2[step, here].astype(jnp.float32)
 
     def round_body(step, carry):
         which = mate_ref[step]
@@ -205,17 +214,23 @@
         choice = choice[0:1]
         inv = whiten(raw.at[step + 1], tt_ref, choice, arrival(step + 1), store_mate)
         scale = inv * (TIME**-0.5)
-        for part, target in ((0, 1 - zlo), (1, zlo)):
-            snd1[step, part] = (quarter(1 - core, target) * scale).astype(jnp.bfloat16)
-            copy_twin(step, part).start()
-            keep[...] = quarter(core, target) * scale
-            copy_twin(step, part).wait_recv()
-            both = keep[...] + rcv1[step, part].astype(jnp.float32)
-            if part == 0:
-                snd2[step] = both.astype(jnp.bfloat16)
-                copy_across(step).start()
-            else:
-                out_ref[step] = both
+        for lag in range(2):
+            here = slice(lag * BLOCK, (lag + 1) * BLOCK)
+            away = product(1 - core, 1 - zlo, lag, 1) * scale
+            snd1[step, 0, here] = away.astype(jnp.bfloat16)
+            copy_twin(step, lag).start()
+        for lag in range(2):
+            here = slice(lag * BLOCK, (lag + 1) * BLOCK)
+            keep[here] = product(core, 1 - zlo, lag, 1) * scale
+            copy_twin(step, lag).wait_recv()
+            both = keep[here] + rcv1[step, 0, here].astype(jnp.float32)
+            snd2[step, here] = both.astype(jnp.bfloat16)
+            copy_across(step, lag).start()
+        snd1[step, 1] = (product(1 - core, zlo, 0, 2) * scale).astype(jnp.bfloat16)
+        copy_twin(step, 2).start()
+        keep[...] = product(core, zlo, 0, 2) * scale
+        copy_twin(step, 2).wait_recv()
+        out_ref[step] = keep[...] + rcv1[step, 1].astype(jnp.float32)
 
         @pl.when(step > 0)
         def _():
@@ -229,21 +244,22 @@
     for unit in range(UNITS):
         bytes_wait(send_sem.at[unit], NBLK - 1)
     for step in range(ROUNDS):
-        copy_twin(step, 0).wait_send()
-        copy_twin(step, 1).wait_send()
-        copy_across(step).wait_send()
+        for part in range(3):
+            copy_twin(step, part).wait_send()
+        for lag in range(2):
+            copy_across(step, lag).wait_send()
 
 
 def prepare_kernel(
-    part_hbm, fir_hbm, bank_hbm, rec_hbm, stage_ref, fir_ref, mate_ref, tt_ref,
-    part_ref, fir_in, bank_ref, rec_ref, sem, rec_sem,
+    small_hbm, bank_hbm, rec_hbm, stage_ref, fir_ref, mate_ref, tt_ref,
+    part_ref, small_ref, bank_ref, rec_ref, sem, rec_sem,
 ):
     slices = rec_sem.shape[0]
     rows = SPAN // slices
     small = [
         pltpu.make_async_copy(source, target, sem.at[i])
         for i, (source, target) in enumerate(
-            ((part_hbm, part_ref), (bank_hbm, bank_ref), (fir_hbm, fir_in))
+            ((small_hbm, part_ref), (bank_hbm, bank_ref), (small_hbm, small_ref))
         )
     ]
     large = [
@@ -257,7 +273,7 @@
     for copy in small:
         copy.wait()
 
-    fir_ref[...] = jnp.broadcast_to(fir_in[...], (8, BLOCK))
+    fir_ref[...] = jnp.broadcast_to(small_ref[ROUNDS : ROUNDS + 1, :], (8, BLOCK))
     me = lax.axis_index("chan")
     for step in range(ROUNDS):
         mate_ref[step] = jnp.full((8, BLOCK), part_ref[step, me], jnp.int32)
@@ -288,9 +304,16 @@
     hbm = pl.BlockSpec(memory_space=pltpu.HBM)
     vmem = pl.BlockSpec(memory_space=pltpu.VMEM)
     slices = 2
+    small = jnp.concatenate(
+        [
+            jnp.pad(partner, ((0, 0), (0, BLOCK - NBLK))),
+            jnp.pad(fir_choice[None, :], ((0, 8 - ROUNDS - 1), (0, 0))),
+        ],
+        axis=0,
+    )
     return pl.pallas_call(
         prepare_kernel,
-        in_specs=[hbm] * 4,
+        in_specs=[hbm] * 3,
         out_specs=[vmem] * 4,
         out_shape=[
             jax.ShapeDtypeStruct((UNITS, NBLK, SPAN, BLOCK), jnp.bfloat16),
@@ -299,8 +322,8 @@
             jax.ShapeDtypeStruct((BANKS * TAPS, 256), jnp.bfloat16),
         ],
         scratch_shapes=[
-            pltpu.SMEM((ROUNDS, NBLK), jnp.int32),
-            pltpu.VMEM((1, BLOCK), jnp.int32),
+            pltpu.SMEM((8, BLOCK), jnp.int32),
+            pltpu.VMEM((8, BLOCK), jnp.int32),
             pltpu.VMEM((BANKS, TAPS), jnp.float32),
             pltpu.VMEM((SPAN, NBLK * BLOCK), jnp.bfloat16),
             pltpu.SemaphoreType.DMA((3,)),
@@ -308,7 +331,7 @@
         ],
         compiler_params=pltpu.CompilerParams(vmem_limit_bytes=14 << 20),
         name="prepare",
-    )(partner, fir_choice[None, :], bank, records)
+    )(small, bank, records)
 
 
 def per_device(records, fir_choice, bank, partner):
@@ -333,7 +356,7 @@
             pltpu.VMEM((ROUNDS, 2 * BLOCK, BLOCK), bf16),
             pltpu.VMEM((ROUNDS, 2 * BLOCK, BLOCK), bf16),
             dma((UNITS,)), dma((UNITS, len(GROUPS))), dma((UNITS,)), dma, dma,
-            dma((ROUNDS, 2)), dma((ROUNDS, 2)), dma((ROUNDS,)), dma((ROUNDS,)),
+            dma((ROUNDS, 3)), dma((ROUNDS, 3)), dma((ROUNDS, 2)), dma((ROUNDS, 2)),
         ],
         compiler_params=pltpu.CompilerParams(
             collective_id=0, has_side_effects=True, vmem_limit_bytes=40 << 20

time: 139 us -> 138 us (level)
    unnamed x8 -> x4, local copies, waits for them, and re-layouts: 3.65 us -> 2.29 us
where the time goes in v3:
time: 138 us; the launch traced here: 137 us
  Pallas kernels  132 us (96%)
  local copies, waits for them, and re-layouts  4.64 us (3%)
    pallas_call x1, Pallas kernels, per_device(): pl.pallas_call(kernel, out_shape=jax.ShapeDtypeStruct((ROUNDS, 2 * BLOCK,...  130 us

profile of v3, /device:TPU:0, one launch (start us, length us, event | category | flops | bytes accessed | tf_op | source)
XLA Modules:
  0.0 137.5 jit_solution(10629741527838632295)
XLA Ops:
  0.0 0.7 pad_add_fusion.small_hbm
  0.7 0.0 copy-start
  0.7 1.6 %copy-done = bf16[1,128,8192]{2,1,0:T(8,128)(2,1)S(1)} copy-done((bf16[1,128,8192]{2,1,0:T(8,128)(2,1)S(1)}, bf16[1,128,8192]{2,1,0:T(8,128)(2,1)}, u32[]{:S(2)}) %copy-start) | copy-done | bytes 2097176
  2.3 0.0 copy-start.1
  2.3 0.7 copy-done.1
  3.0 2.1 %prepare.1 = (bf16[4,32,128,256]{3,2,1,0:T(8,128)(2,1)S(1)}, s32[8,256]{1,0:T(8,128)S(1)}, s32[3,8,256]{2,1,0:T(8,128)S(1)}, bf16[1024,256]{1,0:T(8,128)(2,1)S(1)}) custom-call(s32[8,256]{1,0:T(8,128)S(1)} %pad_add_fusion.small_hbm, f32[16,64]{1,0:T(8,128)S(1)} %copy-done.1, bf16[128,8192]{1,0:T(8,128)(2,1)S(1)} %bitcast.7), custom_call_target="tpu_custom_call" | custom-call | tf_op jit(solution)/shard_map/prepare/pallas_call | solution.py:314
  5.1 130.0 %correlate.1 = f32[3,512,256]{2,1,0:T(8,128)S(1)} custom-call(bf16[4,32,128,256]{3,2,1,0:T(8,128)(2,1)S(1)} %get-tuple-element.9.stage, s32[8,256]{1,0:T(8,128)S(1)} %get-tuple-element.10.fir_ref, s32[3,8,256]{2,1,0:T(8,128)S(1)} %get-tuple-element.11.mate_ref, bf16[1024,256]{1,0:T(8,128)(2,1)S(1)} %get-tuple-element.12.tt_ref), custom_call_target="tpu_custom_call" | custom-call | tf_op jit(solution)/shard_map/correlate/pallas_call | solution.py:342
  135.1 2.4 %copy.7 = f32[3,2,256,256]{3,1,2,0:T(2,128)} copy(f32[3,2,256,256]{3,2,1,0:T(8,128)S(1)} %bitcast.6) | data formatting | bytes 3145728 | tf_op jit(solution)/shard_map/reshape | solution.py:366
Async XLA Ops:
  0.7 1.6 %copy-start = (bf16[1,128,8192]{2,1,0:T(8,128)(2,1)S(1)}, bf16[1,128,8192]{2,1,0:T(8,128)(2,1)}, u32[]{:S(2)}) copy-start(bf16[1,128,8192]{2,1,0:T(8,128)(2,1)} %param.4) | copy-start | bytes 6291460
  2.3 0.7 copy-start.1

commit v4 on v3

--- a/solution.py
+++ b/solution.py
@@ -118,7 +118,7 @@
             device_id_type=MESH,
         ).start()
     choices[me] = fir_ref[...]
-    lax.fori_loop(1, UNITS, send_unit, 0)
+    lax.fori_loop(1, UNITS - 1, send_unit, 0)
 
     def bytes_wait(sem, pieces):
         view = raw.at[0, pl.ds(0, pieces * SPAN)]
@@ -153,6 +153,7 @@
         ownf[pl.ds(base + 8, TAPS)] = values
 
     inv_own = whiten(raw.at[0], tt_ref, fir_ref[0:1], arrival(0), store_own)
+    send_unit(UNITS - 1, 0)
 
     def shift(d, carry):
         base = pl.multiple_of(d * 128, 128)
@@ -250,38 +251,24 @@
             copy_across(step, lag).wait_send()
 
 
-def prepare_kernel(
-    small_hbm, bank_hbm, rec_hbm, stage_ref, fir_ref, mate_ref, tt_ref,
-    part_ref, small_ref, bank_ref, rec_ref, sem, rec_sem,
-):
-    slices = rec_sem.shape[0]
-    rows = SPAN // slices
-    small = [
-        pltpu.make_async_copy(source, target, sem.at[i])
-        for i, (source, target) in enumerate(
-            ((small_hbm, part_ref), (bank_hbm, bank_ref), (small_hbm, small_ref))
-        )
-    ]
-    large = [
-        pltpu.make_async_copy(
-            rec_hbm.at[pl.ds(i * rows, rows)], rec_ref.at[pl.ds(i * rows, rows)], rec_sem.at[i]
-        )
-        for i in range(slices)
-    ]
-    for copy in small + large:
-        copy.start()
-    for copy in small:
-        copy.wait()
-
-    fir_ref[...] = jnp.broadcast_to(small_ref[ROUNDS : ROUNDS + 1, :], (8, BLOCK))
+def prepare_kernel(part_ref, small_ref, rec_ref, stage_ref, fir_ref, mate_ref, tt_ref):
+    for to in range(NBLK):
+        stage_ref[0, to] = rec_ref[:, to * BLOCK : (to + 1) * BLOCK]
+        for step in range(ROUNDS):
+            which = part_ref[BANKS + step, to].astype(jnp.int32)
+            start = pl.multiple_of(which * BLOCK, BLOCK)
+            stage_ref[step + 1, to] = rec_ref[:, pl.ds(start, BLOCK)]
+
+    chosen = small_ref[BANKS + ROUNDS : BANKS + ROUNDS + 1, :].astype(jnp.int32)
+    fir_ref[...] = jnp.broadcast_to(chosen, (8, BLOCK))
     me = lax.axis_index("chan")
     for step in range(ROUNDS):
-        mate_ref[step] = jnp.full((8, BLOCK), part_ref[step, me], jnp.int32)
+        mate_ref[step] = jnp.full((8, BLOCK), part_ref[BANKS + step, me], jnp.float32).astype(jnp.int32)
     tap = lax.broadcasted_iota(jnp.int32, (TAPS, 256), 0)
     lane = lax.broadcasted_iota(jnp.int32, (TAPS, 256), 1)
     flip = (tap + lane == TAPS).astype(jnp.float32)
     turned = jnp.dot(
-        bank_ref[...], flip, precision=lax.Precision.HIGHEST, preferred_element_type=jnp.float32
+        small_ref[0:BANKS, 0:TAPS], flip, precision=lax.Precision.HIGHEST, preferred_element_type=jnp.float32
     )
     for b in range(BANKS):
         row = jnp.broadcast_to(turned[b : b + 1, :], (TAPS, 256))
@@ -290,30 +277,17 @@
         low = (t - high.astype(jnp.float32)).astype(jnp.bfloat16)
         tt_ref[b * TAPS : (b + 1) * TAPS, :] = jnp.concatenate([high, low], axis=1)
 
-    for i in range(slices):
-        large[i].wait()
-        cut = slice(i * rows, (i + 1) * rows)
-        for to in range(NBLK):
-            stage_ref[0, to, cut] = rec_ref[cut, to * BLOCK : (to + 1) * BLOCK]
-            for step in range(ROUNDS):
-                start = pl.multiple_of(part_ref[step, to] * BLOCK, BLOCK)
-                stage_ref[step + 1, to, cut] = rec_ref[cut, pl.ds(start, BLOCK)]
-
 
 def prepare(records, fir_choice, bank, partner):
-    hbm = pl.BlockSpec(memory_space=pltpu.HBM)
+    smem = pl.BlockSpec(memory_space=pltpu.SMEM)
     vmem = pl.BlockSpec(memory_space=pltpu.VMEM)
-    slices = 2
-    small = jnp.concatenate(
-        [
-            jnp.pad(partner, ((0, 0), (0, BLOCK - NBLK))),
-            jnp.pad(fir_choice[None, :], ((0, 8 - ROUNDS - 1), (0, 0))),
-        ],
-        axis=0,
-    )
+    below = 8 - ROUNDS - 1
+    whole = jnp.pad(partner, ((BANKS, 8 - ROUNDS), (0, BLOCK - NBLK)))
+    whole = whole + jnp.pad(fir_choice[None, :], ((BANKS + ROUNDS, below), (0, 0)))
+    small = jnp.pad(bank, ((0, 8), (0, BLOCK - TAPS))) + whole.astype(jnp.float32)
     return pl.pallas_call(
         prepare_kernel,
-        in_specs=[hbm] * 3,
+        in_specs=[smem, vmem, vmem],
         out_specs=[vmem] * 4,
         out_shape=[
             jax.ShapeDtypeStruct((UNITS, NBLK, SPAN, BLOCK), jnp.bfloat16),
@@ -321,17 +295,9 @@
             jax.ShapeDtypeStruct((ROUNDS, 8, BLOCK), jnp.int32),
             jax.ShapeDtypeStruct((BANKS * TAPS, 256), jnp.bfloat16),
         ],
-        scratch_shapes=[
-            pltpu.SMEM((8, BLOCK), jnp.int32),
-            pltpu.VMEM((8, BLOCK), jnp.int32),
-            pltpu.VMEM((BANKS, TAPS), jnp.float32),
-            pltpu.VMEM((SPAN, NBLK * BLOCK), jnp.bfloat16),
-            pltpu.SemaphoreType.DMA((3,)),
-            pltpu.SemaphoreType.DMA((slices,)),
-        ],
         compiler_params=pltpu.CompilerParams(vmem_limit_bytes=14 << 20),
         name="prepare",
-    )(small, bank, records)
+    )(small, small, records)
 
 
 def per_device(records, fir_choice, bank, partner):

time: 138 us -> 137 us (level)
  no operation moved by 1% of the time
where the time goes in v4:
time: 137 us
  Pallas kernels  132 us (96%)
  local copies, waits for them, and re-layouts  3.95 us (3%)
    pallas_call x1, Pallas kernels, per_device(): pl.pallas_call(kernel, out_shape=jax.ShapeDtypeStruct((ROUNDS, 2 * BLOCK,...  130 us

profile of v4, /device:TPU:0, one launch (start us, length us, event | category | flops | bytes accessed | tf_op | source)
XLA Modules:
  0.0 137.0 jit_solution(8202299965529052502)
XLA Ops:
  0.0 0.7 convert_add_fusion.part_ref.small_ref
  0.7 0.0 copy-start
  0.7 1.6 %copy-done = bf16[1,128,8192]{2,1,0:T(8,128)(2,1)S(1)} copy-done((bf16[1,128,8192]{2,1,0:T(8,128)(2,1)S(1)}, bf16[1,128,8192]{2,1,0:T(8,128)(2,1)}, u32[]{:S(2)}) %copy-start) | copy-done | bytes 2097176
  2.3 2.3 %prepare.1 = (bf16[4,32,128,256]{3,2,1,0:T(8,128)(2,1)S(1)}, s32[8,256]{1,0:T(8,128)S(1)}, s32[3,8,256]{2,1,0:T(8,128)S(1)}, bf16[1024,256]{1,0:T(8,128)(2,1)S(1)}) custom-call(f32[24,256]{1,0:T(8,128)S(1)} %convert_add_fusion.part_ref.small_ref, f32[24,256]{1,0:T(8,128)S(1)} %convert_add_fusion.part_ref.small_ref, bf16[128,8192]{1,0:T(8,128)(2,1)S(1)} %bitcast.7), custom_call_target="tpu_custom_call" | custom-call | tf_op jit(solution)/shard_map/prepare/pallas_call | solution.py:288
  4.7 130.0 %correlate.1 = f32[3,512,256]{2,1,0:T(8,128)S(1)} custom-call(bf16[4,32,128,256]{3,2,1,0:T(8,128)(2,1)S(1)} %get-tuple-element.9.stage, s32[8,256]{1,0:T(8,128)S(1)} %get-tuple-element.10.fir_ref, s32[3,8,256]{2,1,0:T(8,128)S(1)} %get-tuple-element.11.mate_ref, bf16[1024,256]{1,0:T(8,128)(2,1)S(1)} %get-tuple-element.12.tt_ref), custom_call_target="tpu_custom_call" | custom-call | tf_op jit(solution)/shard_map/correlate/pallas_call | solution.py:308
  134.6 2.4 %copy.7 = f32[3,2,256,256]{3,1,2,0:T(2,128)} copy(f32[3,2,256,256]{3,2,1,0:T(8,128)S(1)} %bitcast.6) | data formatting | bytes 3145728 | tf_op jit(solution)/shard_map/reshape | solution.py:332
Async XLA Ops:
  0.7 1.6 %copy-start = (bf16[1,128,8192]{2,1,0:T(8,128)(2,1)S(1)}, bf16[1,128,8192]{2,1,0:T(8,128)(2,1)}, u32[]{:S(2)}) copy-start(bf16[1,128,8192]{2,1,0:T(8,128)(2,1)} %param.4) | copy-start | bytes 6291460

commit v5 on v4

--- a/solution.py
+++ b/solution.py
@@ -35,8 +35,8 @@
 MOVES = [(j, move) for j, group in enumerate(GROUPS) for move in group if move != (0, 0, 0)]
 
 
-def whiten(raw_ref, tt_ref, choice, ready, store):
-    def window(w, acc):
+def whiten(raw_ref, tt_ref, choice, ready, last, store):
+    def window(w, acc, weight=None):
         base = pl.multiple_of(w * TAPS, TAPS)
         x = raw_ref[pl.ds(base, 2 * TAPS), :]
         every = jnp.dot(
@@ -48,17 +48,24 @@
         rounded = out.astype(jnp.bfloat16)
         values = rounded.astype(jnp.float32)
         store(base, rounded, values)
-        return acc + (values * values).reshape(TAPS // 8, 8, BLOCK).sum(0)
+        square = (values * values).reshape(TAPS // 8, 8, BLOCK).sum(0)
+        return acc + (square if weight is None else square * weight)
 
     def group(j, acc):
-        for row in ready(j):
+        rows, whole = ready(j)
+        for row in rows:
             for inner in range(1, 8):
                 acc = window(row * 8 + inner, acc)
+        for row in whole:
+            missing = (j == 0) | (row == 4)
+            skip = jnp.where(missing, 1, 0)
+            acc = window(row * 8 + skip, acc, jnp.where(missing, 0.0, 1.0))
         return acc
 
     acc = lax.fori_loop(0, len(GROUPS), group, jnp.zeros((8, BLOCK), jnp.float32))
-    for row in range(NBLK // 4):
-        acc = window(row * 8, acc)
+    first, second = last
+    acc = window(second * 8, window(first * 8, acc))
+    acc = window(32, acc, jnp.where((first == 4) | (second == 4), 0.0, 1.0))
     return lax.rsqrt(acc.sum(0, keepdims=True) * (1.0 / TIME) + 1e-6)
 
 
@@ -124,10 +131,16 @@
         view = raw.at[0, pl.ds(0, pieces * SPAN)]
         pltpu.make_async_copy(view, view, sem).wait()
 
+    def rows_of(j):
+        dz, dy = j // 2, j % 2
+        first = ((mz + dz) % 2) * 4 + (my + 4 - turn * dy) % 4
+        second = ((mz + 1 - dz) % 2) * 4 + (my + 8 - turn * (dy + 2)) % 4
+        return first, second
+
+    last = rows_of((1 - core) * 3)
+
     def arrival(unit):
         def ready(j):
-            dz, dy = j // 2, j % 2
-
             @pl.when(j == 0)
             def _():
                 bytes_wait(recv_sem.at[unit, j], 7)
@@ -137,9 +150,8 @@
             def _():
                 bytes_wait(recv_sem.at[unit, j], 8)
 
-            first = ((mz + dz) % 2) * 4 + (my + 4 - turn * dy) % 4
-            second = ((mz + 1 - dz) % 2) * 4 + (my + 8 - turn * (dy + 2)) % 4
-            return first, second
+            before = jnp.where(core == 0, jnp.maximum(j - 1, 0), j)
+            return rows_of(j), rows_of(before)
 
         return ready
 
@@ -152,7 +164,7 @@
     def store_own(base, rounded, values):
         ownf[pl.ds(base + 8, TAPS)] = values
 
-    inv_own = whiten(raw.at[0], tt_ref, fir_ref[0:1], arrival(0), store_own)
+    inv_own = whiten(raw.at[0], tt_ref, fir_ref[0:1], arrival(0), last, store_own)
     send_unit(UNITS - 1, 0)
 
     def shift(d, carry):
@@ -213,7 +225,7 @@
         for block in range(1, NBLK):
             choice = jnp.where(which == block, choices[block], choice)
         choice = choice[0:1]
-        inv = whiten(raw.at[step + 1], tt_ref, choice, arrival(step + 1), store_mate)
+        inv = whiten(raw.at[step + 1], tt_ref, choice, arrival(step + 1), last, store_mate)
         scale = inv * (TIME**-0.5)
         for lag in range(2):
             here = slice(lag * BLOCK, (lag + 1) * BLOCK)

time: 137 us -> 138 us (level)
  no operation moved by 1% of the time
where the time goes in v5:
time: 138 us
  Pallas kernels  133 us (96%)
  local copies, waits for them, and re-layouts  3.95 us (3%)
    pallas_call x1, Pallas kernels, per_device(): pl.pallas_call(kernel, out_shape=jax.ShapeDtypeStruct((ROUNDS, 2 * BLOCK,...  131 us

profile of v5, /device:TPU:0, one launch (start us, length us, event | category | flops | bytes accessed | tf_op | source)
XLA Modules:
  0.0 137.6 jit_solution(10174304257111851237)
XLA Ops:
  0.0 0.7 convert_add_fusion.part_ref.small_ref
  0.7 0.0 copy-start
  0.7 1.6 %copy-done = bf16[1,128,8192]{2,1,0:T(8,128)(2,1)S(1)} copy-done((bf16[1,128,8192]{2,1,0:T(8,128)(2,1)S(1)}, bf16[1,128,8192]{2,1,0:T(8,128)(2,1)}, u32[]{:S(2)}) %copy-start) | copy-done | bytes 2097176
  2.3 2.4 %prepare.1 = (bf16[4,32,128,256]{3,2,1,0:T(8,128)(2,1)S(1)}, s32[8,256]{1,0:T(8,128)S(1)}, s32[3,8,256]{2,1,0:T(8,128)S(1)}, bf16[1024,256]{1,0:T(8,128)(2,1)S(1)}) custom-call(f32[24,256]{1,0:T(8,128)S(1)} %convert_add_fusion.part_ref.small_ref, f32[24,256]{1,0:T(8,128)S(1)} %convert_add_fusion.part_ref.small_ref, bf16[128,8192]{1,0:T(8,128)(2,1)S(1)} %bitcast.7), custom_call_target="tpu_custom_call" | custom-call | tf_op jit(solution)/shard_map/prepare/pallas_call | solution.py:300
  4.7 130.5 %correlate.1 = f32[3,512,256]{2,1,0:T(8,128)S(1)} custom-call(bf16[4,32,128,256]{3,2,1,0:T(8,128)(2,1)S(1)} %get-tuple-element.9.stage, s32[8,256]{1,0:T(8,128)S(1)} %get-tuple-element.10.fir_ref, s32[3,8,256]{2,1,0:T(8,128)S(1)} %get-tuple-element.11.mate_ref, bf16[1024,256]{1,0:T(8,128)(2,1)S(1)} %get-tuple-element.12.tt_ref), custom_call_target="tpu_custom_call" | custom-call | tf_op jit(solution)/shard_map/correlate/pallas_call | solution.py:320
  135.2 2.4 %copy.7 = f32[3,2,256,256]{3,1,2,0:T(2,128)} copy(f32[3,2,256,256]{3,2,1,0:T(8,128)S(1)} %bitcast.6) | data formatting | bytes 3145728 | tf_op jit(solution)/shard_map/reshape | solution.py:344
Async XLA Ops:
  0.7 1.6 %copy-start = (bf16[1,128,8192]{2,1,0:T(8,128)(2,1)S(1)}, bf16[1,128,8192]{2,1,0:T(8,128)(2,1)}, u32[]{:S(2)}) copy-start(bf16[1,128,8192]{2,1,0:T(8,128)(2,1)} %param.4) | copy-start | bytes 6291460
